TPU v7x, 32 devices: a whole 2x2x4 slice. The times are simulated.
32 devices in a mesh: dp: 8 (over z, x), seq: 4 (over y, core).
Axes of the slice: x: 2, y: 2, z: 4, core: 2. Of those that a mesh axis runs over, the one named last changes fastest.
Arguments:
- short_in: bfloat16 [2, 32, 256, 768], P(None, 'dp', 'seq'), may hold values from -6 to 6
- long_in: bfloat16 [2, 16, 512, 768], P(None, 'dp', 'seq'), may hold values from -6 to 6
- short_cot: bfloat16 [2, 32, 256, 768], P(None, 'dp', 'seq'), may hold values from -6 to 6
- long_cot: bfloat16 [2, 16, 512, 768], P(None, 'dp', 'seq'), may hold values from -6 to 6
- short_len: int32 [2, 8, 4], P(None, 'dp'), may hold values from 0 to 256, as said below
- long_len: int32 [2, 8, 2], P(None, 'dp'), may hold values from 0 to 512, as said below
- wide_master: float32 [768, 6144], P('dp')
- down_master: float32 [3072, 768], P('dp'), may hold values from -0.109375 to 0.109375
- vector_master: float32 [768, 12], P('dp')
- wide_moment: float32 [768, 6144], P('dp'), may hold values from -256 to 256
- down_moment: float32 [3072, 768], P('dp'), may hold values from -256 to 256
- vector_moment: float32 [768, 12], P('dp'), may hold values from -256 to 256
- wide_average: float32 [768, 6144], P('dp'), may hold values from -0.21875 to 0.21875
- down_average: float32 [3072, 768], P('dp'), may hold values from -0.109375 to 0.109375
- vector_average: float32 [768, 12], P('dp'), may hold values from -6 to 6
Outputs:
- short_out: bfloat16 [2, 32, 256, 768], P(None, 'dp', 'seq')
- long_out: bfloat16 [2, 16, 512, 768], P(None, 'dp', 'seq')
- short_back: bfloat16 [2, 32, 256, 768], P(None, 'dp', 'seq')
- long_back: bfloat16 [2, 16, 512, 768], P(None, 'dp', 'seq')
- wide_grad: float32 [768, 6144], P('dp')
- down_grad: float32 [3072, 768], P('dp')
- vector_grad: float32 [768, 12], P('dp')
- wide_velocity: float32 [768, 6144], P('dp')
- down_velocity: float32 [3072, 768], P('dp')
- vector_velocity: float32 [768, 12], P('dp')
- wide_averaged: float32 [768, 6144], P('dp')
- down_averaged: float32 [3072, 768], P('dp')
- vector_averaged: float32 [768, 12], P('dp')
- wide_updated: float32 [768, 6144], P('dp')
- down_updated: float32 [3072, 768], P('dp')
- vector_updated: float32 [768, 12], P('dp')
- wide_copy: bfloat16 [768, 6144], P('dp')
- down_copy: bfloat16 [3072, 768], P('dp')
- vector_copy: bfloat16 [768, 12], P('dp')
Inputs may be any that keep to these rules, and one draw needn't show every extreme that they name: `short_len`: 0 marks an empty slot; in each micro-batch every index of dp has at least half of its slots live and one sequence of exactly 256 tokens. `long_len`: 0 marks an empty slot; in each micro-batch every index of dp has at least half of its slots live and one sequence of exactly 512 tokens.
All inputs are finite; a program needn't handle non-finite values.
Results may differ from a plain program's by a relative error of at most 0.015.
Values may be sent and summed in bfloat16 or wider, within the bound.
A program may use at most 256 MiB of HBM per device.

v0:
```python
import jax
import jax.numpy as jnp
from jax import lax
from jax.sharding import PartitionSpec as P

D = 768
HEAD_DIM = 64
FF = 3072
norm_eps = 1e-12
mask_fill = -10000.0
learning_rate = 0.0002
momentum_rate = 0.9
decay_weight = 0.0001
average_rate = 0.9


def norm_forward(inputs, gain, shift):
    centred = inputs - jnp.mean(inputs, axis=-1, keepdims=True)
    inverse = lax.rsqrt(jnp.mean(centred * centred, axis=-1, keepdims=True) + norm_eps)
    normed = centred * inverse
    return (normed * gain + shift, normed, inverse)


def norm_backward(grad_out, normed, inverse, gain):
    scaled = grad_out * gain
    grad_in = inverse * (
        scaled
        - jnp.mean(scaled, axis=-1, keepdims=True)
        - normed * jnp.mean(scaled * normed, axis=-1, keepdims=True)
    )
    return (grad_in, jnp.sum(grad_out * normed, axis=0), jnp.sum(grad_out, axis=0))


def transpose_dot(left, right):
    return jnp.einsum("ra,rb->ab", left, right, preferred_element_type=jnp.float32)


def right_dot(left, right):
    return jnp.einsum("ra,ba->rb", left, right, preferred_element_type=jnp.float32)


def weight_grads(factor_list):
    products = []
    for kind in range(4):
        left = jnp.concatenate([factors[kind][0] for factors in factor_list], axis=0)
        right = jnp.concatenate([factors[kind][1] for factors in factor_list], axis=0)
        products.append(transpose_dot(left, right))
    return products


def micro_step(tokens, cotangent, lengths, weights, spread):
    wide_w, down_w, vector_w = weights
    seq_count, local_len, model_width = tokens.shape
    row_count = seq_count * local_len
    parts_count = lax.axis_size("seq") if spread else 1
    full_len = local_len * parts_count
    head_width = model_width // parts_count
    local_heads = head_width // HEAD_DIM
    vector = vector_w.astype(jnp.float32)
    flat_rows = tokens.reshape(row_count, model_width)
    proj_bias = jnp.concatenate(
        [vector[:, 0], jnp.zeros((model_width,), jnp.float32), vector[:, 1]]
    )
    projected = (
        jnp.dot(flat_rows, wide_w[:, : 3 * model_width], preferred_element_type=jnp.float32)
        + proj_bias
    )
    stacked = projected.astype(jnp.bfloat16).reshape(seq_count, local_len, 3, model_width)
    if spread:
        headed = lax.all_to_all(stacked, "seq", split_axis=3, concat_axis=1, tiled=True)
    else:
        headed = stacked
    headed = headed.reshape(seq_count, full_len, 3, local_heads, HEAD_DIM)
    queries = headed[:, :, 0]
    key_rows = headed[:, :, 1]
    values = headed[:, :, 2]
    key_live = (jnp.arange(full_len)[None, :] < lengths[:, None])[:, None, None, :]
    score_scale = HEAD_DIM ** (-0.5)
    raw_scores = (
        jnp.einsum("bqhd,bkhd->bhqk", queries, key_rows, preferred_element_type=jnp.float32)
        * score_scale
    )
    scores = jnp.where(key_live, raw_scores, mask_fill)
    row_top = jnp.max(scores, axis=-1, keepdims=True)
    exponent = jnp.exp(scores - row_top)
    row_total = jnp.sum(exponent, axis=-1, keepdims=True)
    log_total = row_top + jnp.log(row_total)
    probs = (exponent / row_total).astype(jnp.bfloat16)
    attended = jnp.einsum("bhqk,bkhd->bqhd", probs, values, preferred_element_type=jnp.float32)
    attended = attended.astype(jnp.bfloat16).reshape(seq_count, full_len, head_width)
    if spread:
        gathered = lax.all_to_all(attended, "seq", split_axis=1, concat_axis=2, tiled=True)
    else:
        gathered = attended
    attn_rows = gathered.reshape(row_count, model_width)
    branch = (
        jnp.dot(
            attn_rows,
            wide_w[:, 3 * model_width : 4 * model_width],
            preferred_element_type=jnp.float32,
        )
        + vector[:, 2]
    )
    first, normed_one, inverse_one = norm_forward(
        flat_rows.astype(jnp.float32) + branch, vector[:, 3], vector[:, 4]
    )
    first_low = first.astype(jnp.bfloat16)
    bias_one = jnp.transpose(vector[:, 8:]).reshape(-1)
    inner_pre = (
        jnp.dot(first_low, wide_w[:, 4 * model_width :], preferred_element_type=jnp.float32)
        + bias_one
    )
    active = jax.nn.gelu(inner_pre, approximate=False).astype(jnp.bfloat16)
    branch_two = jnp.dot(active, down_w, preferred_element_type=jnp.float32) + vector[:, 5]
    result, normed_two, inverse_two = norm_forward(first + branch_two, vector[:, 6], vector[:, 7])
    output = result.astype(jnp.bfloat16).reshape(tokens.shape)
    offset = lax.axis_index("seq") * local_len if spread else 0
    position = offset + jnp.arange(local_len)
    live_rows = (position[None, :] < lengths[:, None]).astype(jnp.float32).reshape(row_count, 1)
    grad_out = cotangent.reshape(row_count, model_width).astype(jnp.float32) * live_rows
    grad_mid, grad_gain_two, grad_shift_two = norm_backward(
        grad_out, normed_two, inverse_two, vector[:, 6]
    )
    grad_mid_low = grad_mid.astype(jnp.bfloat16)
    grad_active = right_dot(grad_mid_low, down_w)
    normal_cdf = 0.5 * (1.0 + jax.scipy.special.erf(inner_pre * 0.5**0.5))
    normal_pdf = jnp.exp(-0.5 * inner_pre * inner_pre) * (2.0 * jnp.pi) ** (-0.5)
    grad_inner = (grad_active * (normal_cdf + inner_pre * normal_pdf)).astype(jnp.bfloat16)
    grad_first = grad_mid + right_dot(grad_inner, wide_w[:, 4 * model_width :])
    grad_resid, grad_gain_one, grad_shift_one = norm_backward(
        grad_first, normed_one, inverse_one, vector[:, 3]
    )
    grad_resid_low = grad_resid.astype(jnp.bfloat16)
    grad_attended = right_dot(grad_resid_low, wide_w[:, 3 * model_width : 4 * model_width])
    grad_attended = grad_attended.astype(jnp.bfloat16).reshape(seq_count, local_len, model_width)
    if spread:
        grad_headed = lax.all_to_all(grad_attended, "seq", split_axis=2, concat_axis=1, tiled=True)
    else:
        grad_headed = grad_attended
    grad_heads = grad_headed.reshape(seq_count, full_len, local_heads, HEAD_DIM)
    again_scores = jnp.where(
        key_live,
        jnp.einsum("bqhd,bkhd->bhqk", queries, key_rows, preferred_element_type=jnp.float32)
        * score_scale,
        mask_fill,
    )
    prob_exact = jnp.exp(again_scores - log_total)
    grad_probs = jnp.einsum(
        "bqhd,bkhd->bhqk", grad_heads, values, preferred_element_type=jnp.float32
    )
    grad_scores = prob_exact * (
        grad_probs - jnp.sum(prob_exact * grad_probs, axis=-1, keepdims=True)
    )
    grad_scores = jnp.where(key_live, grad_scores, 0.0).astype(jnp.bfloat16)
    grad_query = (
        jnp.einsum("bhqk,bkhd->bqhd", grad_scores, key_rows, preferred_element_type=jnp.float32)
        * score_scale
    )
    grad_key = (
        jnp.einsum("bhqk,bqhd->bkhd", grad_scores, queries, preferred_element_type=jnp.float32)
        * score_scale
    )
    grad_value = jnp.einsum(
        "bhqk,bqhd->bkhd", probs, grad_heads, preferred_element_type=jnp.float32
    )
    grad_stack = jnp.stack([grad_query, grad_key, grad_value], axis=2)
    grad_stack = grad_stack.astype(jnp.bfloat16).reshape(seq_count, full_len, 3, head_width)
    if spread:
        grad_local = lax.all_to_all(grad_stack, "seq", split_axis=1, concat_axis=3, tiled=True)
    else:
        grad_local = grad_stack
    grad_proj = grad_local.reshape(row_count, 3 * model_width)
    grad_input = grad_resid + right_dot(grad_proj, wide_w[:, : 3 * model_width])
    back = grad_input.astype(jnp.bfloat16).reshape(tokens.shape)
    proj_sums = jnp.sum(grad_proj.astype(jnp.float32), axis=0)
    grad_bias_one = jnp.sum(grad_inner.astype(jnp.float32), axis=0)
    grad_columns = jnp.stack(
        [
            proj_sums[:model_width],
            proj_sums[2 * model_width :],
            jnp.sum(grad_resid_low.astype(jnp.float32), axis=0),
            grad_gain_one,
            grad_shift_one,
            jnp.sum(grad_mid_low.astype(jnp.float32), axis=0),
            grad_gain_two,
            grad_shift_two,
        ],
        axis=1,
    )
    grad_vector = jnp.concatenate(
        [grad_columns, jnp.transpose(grad_bias_one.reshape(-1, model_width))], axis=1
    )
    factors = (
        (flat_rows, grad_proj),
        (attn_rows, grad_resid_low),
        (first_low, grad_inner),
        (active, grad_mid_low),
    )
    return (output, back, factors, grad_vector)


def update(master, reduced_grad, moment, average):
    step_grad = reduced_grad + decay_weight * master
    velocity = momentum_rate * moment + step_grad
    updated = master - learning_rate * (step_grad + momentum_rate * velocity)
    averaged = average_rate * average + (1.0 - average_rate) * updated
    return (velocity, averaged, updated, updated.astype(jnp.bfloat16))


def body(
    short_in,
    long_in,
    short_cot,
    long_cot,
    short_len,
    long_len,
    wide_master,
    down_master,
    vector_master,
    wide_moment,
    down_moment,
    vector_moment,
    wide_average,
    down_average,
    vector_average,
):
    weights = (
        lax.all_gather(wide_master.astype(jnp.bfloat16), "dp", axis=0, tiled=True),
        lax.all_gather(down_master.astype(jnp.bfloat16), "dp", axis=0, tiled=True),
        lax.all_gather(vector_master.astype(jnp.bfloat16), "dp", axis=0, tiled=True),
    )
    own_rows = wide_master.shape[0]
    sums = (
        jnp.zeros((own_rows, 3 * D), jnp.float32),
        jnp.zeros((own_rows, D), jnp.float32),
        jnp.zeros((own_rows, FF), jnp.float32),
        jnp.zeros(down_master.shape, jnp.float32),
        jnp.zeros(vector_master.shape, jnp.float32),
    )
    factor_list = []
    vector_total = jnp.zeros(weights[2].shape, jnp.float32)
    bucket_results = []
    for bucket_index, (tokens, cotangent, lengths) in enumerate(
        ((short_in, short_cot, short_len), (long_in, long_cot, long_len))
    ):
        outputs = []
        backs = []
        for micro_index in range(tokens.shape[0]):
            micro_tokens = tokens[micro_index]
            micro_cot = cotangent[micro_index]
            micro_len = lengths[micro_index, 0]
            if bucket_index == 0:
                own_count = micro_tokens.shape[0] // lax.axis_size("seq")
                whole_tokens, whole_cot = (
                    lax.all_to_all(micro_tokens, "seq", split_axis=0, concat_axis=1, tiled=True),
                    lax.all_to_all(micro_cot, "seq", split_axis=0, concat_axis=1, tiled=True),
                )
                own_len = lax.dynamic_slice_in_dim(
                    micro_len, lax.axis_index("seq") * own_count, own_count
                )
                whole_out, whole_back, factors, grad_vector = micro_step(
                    whole_tokens, whole_cot, own_len, weights, False
                )
                output, back = (
                    lax.all_to_all(whole_out, "seq", split_axis=1, concat_axis=0, tiled=True),
                    lax.all_to_all(whole_back, "seq", split_axis=1, concat_axis=0, tiled=True),
                )
            else:
                output, back, factors, grad_vector = micro_step(
                    micro_tokens, micro_cot, micro_len, weights, True
                )
            factor_list.append(factors)
            vector_total = vector_total + grad_vector
            outputs.append(output)
            backs.append(back)
        bucket_results.append((jnp.stack(outputs), jnp.stack(backs)))
    products = weight_grads(factor_list)
    sums = (
        lax.psum_scatter(products[0], "dp", scatter_dimension=0, tiled=True),
        lax.psum_scatter(products[1], "dp", scatter_dimension=0, tiled=True),
        lax.psum_scatter(products[2], "dp", scatter_dimension=0, tiled=True),
        lax.psum_scatter(products[3], "dp", scatter_dimension=0, tiled=True),
        lax.psum_scatter(vector_total, "dp", scatter_dimension=0, tiled=True),
    )
    reduced = (
        lax.psum(sums[0].astype(jnp.bfloat16), "seq").astype(jnp.float32),
        lax.psum(sums[1].astype(jnp.bfloat16), "seq").astype(jnp.float32),
        lax.psum(sums[2].astype(jnp.bfloat16), "seq").astype(jnp.float32),
        lax.psum(sums[3].astype(jnp.bfloat16), "seq").astype(jnp.float32),
        lax.psum(sums[4].astype(jnp.bfloat16), "seq").astype(jnp.float32),
    )
    wide_reduced = jnp.concatenate([reduced[0], reduced[1], reduced[2]], axis=1)
    down_reduced = reduced[3]
    vector_reduced = reduced[4]
    wide_new = update(wide_master, wide_reduced, wide_moment, wide_average)
    down_new = update(down_master, down_reduced, down_moment, down_average)
    vector_new = update(vector_master, vector_reduced, vector_moment, vector_average)
    return (
        bucket_results[0][0],
        bucket_results[1][0],
        bucket_results[0][1],
        bucket_results[1][1],
        wide_reduced,
        down_reduced,
        vector_reduced,
        wide_new[0],
        down_new[0],
        vector_new[0],
        wide_new[1],
        down_new[1],
        vector_new[1],
        wide_new[2],
        down_new[2],
        vector_new[2],
        wide_new[3],
        down_new[3],
        vector_new[3],
    )


def solution(mesh):
    return jax.shard_map(
        body,
        mesh=mesh,
        in_specs=(
            P(None, "dp", "seq", None),
            P(None, "dp", "seq", None),
            P(None, "dp", "seq", None),
            P(None, "dp", "seq", None),
            P(None, "dp", None),
            P(None, "dp", None),
            P("dp", None),
            P("dp", None),
            P("dp", None),
            P("dp", None),
            P("dp", None),
            P("dp", None),
            P("dp", None),
            P("dp", None),
            P("dp", None),
        ),
        out_specs=(
            P(None, "dp", "seq", None),
            P(None, "dp", "seq", None),
            P(None, "dp", "seq", None),
            P(None, "dp", "seq", None),
            P("dp", None),
            P("dp", None),
            P("dp", None),
            P("dp", None),
            P("dp", None),
            P("dp", None),
            P("dp", None),
            P("dp", None),
            P("dp", None),
            P("dp", None),
            P("dp", None),
            P("dp", None),
            P("dp", None),
            P("dp", None),
            P("dp", None),
        ),
        check_vma=False,
    )
```

profile of v0, /device:TPU:0, one launch (start us, length us, event | category | flops | bytes accessed | tf_op | source)
XLA Modules:
  0.0 1123.6 jit_solution(16164182160932773514)
XLA Ops:
  11.2 4.4 all-to-all-start.8
  20.8 32.3 %all-gather = bf16[8,96,12]{1,2,0:T(8,128)(2,1)S(1)} all-gather(bf16[1,96,12]{1,2,0:T(8,128)(2,1)S(1)} %convert_bitcast_fusion), channel_id=1, replica_groups=mesh['dp'=8,'seq'=4] {'dp'}, dimensions={0}, use_global_device_ids=true | all-gather | bytes 20736 | tf_op jit(solution)/shard_map/all_gather | solution.py:230
  58.9 3.5 all-to-all-start.10
  65.1 4.7 all-to-all-done.10
  69.8 3.5 all-to-all-start.2
  75.5 5.2 all-to-all-done.2
  80.7 3.5 all-to-all-start
  84.2 67.5 %all-gather.4.cloned.1.call-done = bf16[768,6144]{1,0:T(8,128)(2,1)} async-done(((bf16[96,6144]{1,0:T(8,128)(2,1)}), bf16[768,6144]{1,0:T(8,128)(2,1)}) %all-gather.4.cloned.1.call-update) | async-done | bytes 9437200 | tf_op jit(solution)/shard_map/all_gather | solution.py:228
  155.4 3.6 fusion.42
  160.9 5.0 copy.368
  170.9 5.0 copy.375
  175.8 4.8 all-to-all-start.4
  180.7 4.1 fusion.40
  196.9 3.7 all-to-all-start.6
  209.6 6.8 all-to-all-done.6
  230.8 3.5 all-to-all-start.7
  245.4 3.7 all-to-all-start.5
  251.7 6.2 all-to-all-done.5
  266.9 10.8 fusion.66
  277.8 4.5 fusion.382
  282.6 9.5 fusion.63
  294.9 10.0 fusion.69
  306.7 9.6 fusion.60
  343.8 3.6 convert_reduce_fusion.11
  359.8 4.1 all-to-all-start.14
  372.6 4.0 fusion.177
  376.7 6.7 fusion.241
  383.4 6.7 fusion.247
  393.3 4.1 all-to-all-start.12
  414.6 5.0 fusion.316
  419.5 11.7 %fusion.269 = bf16[2,3,64,512]{3,2,1,0:T(8,128)(2,1)S(1)} fusion(f32[2,3,512,512]{2,3,1,0:T(8,128)} %fusion.316, f32[2,3,512,512]{2,3,1,0:T(8,128)} %copy-done.1, f32[2,3,512]{2,1,0:T(4,128)S(1)} %copy-done.104, pred[2,512]{1,0:T(4,128)(4,1)S(1)} %copy-done.85, bf16[2,512,3,3,64]{1,4,3,0,2:T(8,128)(2,1)S(1)} %copy-done.18), kind=kOutput, calls=%fused_computation.309 | convolution fusion | flops 219024896 | bytes 25989120 | tf_op jit(solution)/shard_map/bhqk,bkhd->bqhd/dot_general | solution.py:156
  431.7 11.9 %fusion.266 = bf16[2,3,64,512]{3,2,1,0:T(8,128)(2,1)S(1)} fusion(f32[2,3,512,512]{2,3,1,0:T(8,128)} %fusion.316, f32[2,3,512,512]{2,3,1,0:T(8,128)} %copy-done.1, f32[2,3,512]{2,1,0:T(4,128)S(1)} %copy-done.104, pred[2,512]{1,0:T(4,128)(4,1)S(1)} %copy-done.85, bf16[2,512,3,3,64]{1,4,3,0,2:T(8,128)(2,1)S(1)} %copy-done.18), kind=kOutput, calls=%fused_computation.308 | convolution fusion | flops 219024896 | bytes 25989120 | tf_op jit(solution)/shard_map/bhqk,bqhd->bkhd/dot_general | solution.py:160
  447.3 4.0 all-to-all-start.13
  451.4 3.7 fusion.318
  455.0 11.6 %fusion.275 = bf16[2,3,64,512]{3,2,1,0:T(8,128)(2,1)S(1)} fusion(f32[2,3,512,512]{2,3,1,0:T(8,128)} %fusion.318, f32[2,3,512,512]{2,3,1,0:T(8,128)} %copy-done, f32[2,3,512]{2,1,0:T(4,128)} %log_add_fusion, pred[2,512]{1,0:T(4,128)(4,1)S(1)} %copy-done.83, bf16[2,512,3,3,64]{1,4,3,0,2:T(8,128)(2,1)S(1)} %copy-done.17), kind=kOutput, calls=%fused_computation.311 | convolution fusion | flops 219024896 | bytes 25989120 | tf_op jit(solution)/shard_map/bhqk,bkhd->bqhd/dot_general | solution.py:156
  467.7 11.8 %fusion.272 = bf16[2,3,64,512]{3,2,1,0:T(8,128)(2,1)S(1)} fusion(f32[2,3,512,512]{2,3,1,0:T(8,128)} %fusion.318, f32[2,3,512,512]{2,3,1,0:T(8,128)} %copy-done, f32[2,3,512]{2,1,0:T(4,128)} %log_add_fusion, pred[2,512]{1,0:T(4,128)(4,1)S(1)} %copy-done.83, bf16[2,512,3,3,64]{1,4,3,0,2:T(8,128)(2,1)S(1)} %copy-done.17), kind=kOutput, calls=%fused_computation.310 | convolution fusion | flops 219024896 | bytes 25989120 | tf_op jit(solution)/shard_map/bhqk,bqhd->bkhd/dot_general | solution.py:160
  480.6 4.9 pad_maximum_fusion.1
  485.5 4.4 all-to-all-start.15
  492.2 6.9 fusion.253
  499.1 6.9 fusion.259
  515.0 3.6 copy.413
  521.0 7.7 fusion.28
  528.8 9.9 fusion.4
  538.8 10.3 fusion.12
  552.2 4.7 reduce.54
  558.7 4.1 all-to-all-start.3
  578.0 4.7 reduce.55
  607.6 4.4 all-to-all-start.1
  612.0 3.7 fusion.282
  617.1 4.7 reduce.56
  623.6 4.1 all-to-all-start.11
  627.8 3.7 fusion.283
  632.9 4.7 reduce.57
  639.5 4.1 all-to-all-start.9
  655.1 3.3 reshape.972
  665.6 3.3 reshape.976
  685.2 4.4 fusion.280
  693.2 130.2 %reduce-scatter.12.cloned.1.call-done = f32[96,3072]{1,0:T(8,128)} async-done(((f32[768,3072]{1,0:T(8,128)}), f32[96,3072]{1,0:T(8,128)}) %reduce-scatter.12.cloned.1.call-update) | async-done | bytes 1179664 | tf_op jit(solution)/shard_map/reduce_scatter | solution.py:281
  825.6 164.3 %reduce-scatter.14.cloned.1.call-done = f32[384,768]{1,0:T(8,128)} async-done(((f32[3072,768]{1,0:T(8,128)}), f32[384,768]{1,0:T(8,128)}) %reduce-scatter.14.cloned.1.call-update) | async-done | bytes 1179664 | tf_op jit(solution)/shard_map/reduce_scatter | solution.py:282
  992.1 3.5 fusion.281
  996.6 58.1 %reduce-scatter.16.cloned.1.call-done = f32[96,12]{1,0:T(8,128)} async-done(((f32[768,12]{1,0:T(8,128)}), f32[96,12]{1,0:T(8,128)}) %reduce-scatter.16.cloned.1.call-update) | async-done | bytes 4624
  1055.5 5.7 psum.39
  1063.1 41.8 %all-reduce.3.cloned.1.call-done = (bf16[96,3072]{1,0:T(8,128)(2,1)}, bf16[96,768]{1,0:T(8,128)(2,1)}, bf16[96,2304]{1,0:T(8,128)(2,1)}, bf16[384,768]{1,0:T(8,128)(2,1)}) async-done(((bf16[96,3072]{1,0:T(8,128)(2,1)}, bf16[96,768]{1,0:T(8,128)(2,1)}, bf16[96,2304]{1,0:T(8,128)(2,1)}, bf16[384,768]{1,0:T(8,128)(2,1)}), (bf16[96,3072]{1,0:T(8,128)(2,1)}, bf16[96,768]{1,0:T(8,128)(2,1)}, ...) | async-done | bytes 1769488 | tf_op jit(solution)/shard_map/psum | solution.py:288
  1110.8 3.4 fusion.366
  (572 shorter events, 287.3 us)
Async XLA Ops:
  7.2 144.5 %all-gather.4.cloned.1.call-start = ((), (), s32[]{:S(2)}) async-start(), calls=%async_computation.21 | async-start | bytes 10616832 | tf_op jit(solution)/shard_map/all_gather | solution.py:228
  10.2 10.6 copy-start.89
  10.2 43.7 %copy-start.132 = (s32[2,1,2]{2,1,0:T(1,128)S(1)}, s32[2,1,2]{2,1,0:T(1,128)}, u32[]{:S(2)}) copy-start(s32[2,1,2]{2,1,0:T(1,128)} %param.20) | copy-start | bytes 52
  10.2 45.1 %copy-start.14 = (bf16[2,2,128,768]{3,2,1,0:T(8,128)(2,1)S(1)}, bf16[2,2,128,768]{3,2,1,0:T(8,128)(2,1)}, u32[]{:S(2)}) copy-start(bf16[2,2,128,768]{3,2,1,0:T(8,128)(2,1)} %param.18) | copy-start | bytes 2359300
  11.2 46.8 %copy-start.44 = (bf16[2,4,64,768]{3,2,1,0:T(8,128)(2,1)S(1)}, bf16[2,4,64,768]{3,2,1,0:T(8,128)(2,1)}, u32[]{:S(2)}) copy-start(bf16[2,4,64,768]{3,2,1,0:T(8,128)(2,1)} %param.15) | copy-start | bytes 2359300
  11.2 47.7 %all-to-all-start.8 = ((bf16[4,64,768]{2,1,0:T(8,128)(2,1)}), bf16[4,64,768]{2,1,0:T(8,128)(2,1)S(1)}, u32[]{:S(2)}, u32[]{:S(2)}) async-start(bf16[4,64,768]{2,1,0:T(8,128)(2,1)} %get-tuple-element.113), calls=%async_computation.8 | async-start | bytes 786432 | tf_op jit(solution)/shard_map/all_to_all | solution.py:256
  15.5 262.2 %all-gather.6.cloned.1.call-start = ((), (), s32[]{:S(2)}) async-start(), calls=%async_computation.22 | async-start | bytes 5308416 | tf_op jit(solution)/shard_map/all_gather | solution.py:229
  16.4 47.7 %copy-start.45 = (bf16[2,2,128,768]{3,2,1,0:T(8,128)(2,1)S(1)}, bf16[2,2,128,768]{3,2,1,0:T(8,128)(2,1)}, u32[]{:S(2)}) copy-start(bf16[2,2,128,768]{3,2,1,0:T(8,128)(2,1)} %param.16) | copy-start | bytes 2359300
  53.9 20.3 %copy-start.75 = (f32[768]{0:T(1024)}, f32[768]{0:T(1024)S(1)}, u32[]{:S(2)}) copy-start(f32[768]{0:T(1024)S(1)} %get-tuple-element.53) | copy-start | bytes 9220
  58.9 92.7 %copy-start.25 = (bf16[4,64,768]{2,1,0:T(8,128)(2,1)}, bf16[4,64,768]{2,1,0:T(8,128)(2,1)S(1)}, u32[]{:S(2)}) copy-start(bf16[4,64,768]{2,1,0:T(8,128)(2,1)S(1)} %all-to-all-done.8) | copy-start | bytes 1179652
  58.9 10.9 all-to-all-start.10
  69.8 10.9 all-to-all-start.2
  80.7 74.1 %copy-start.65 = (bf16[4,64,768]{2,1,0:T(8,128)(2,1)}, bf16[4,64,768]{2,1,0:T(8,128)(2,1)S(1)}, u32[]{:S(2)}) copy-start(bf16[4,64,768]{2,1,0:T(8,128)(2,1)S(1)} %all-to-all-done.2) | copy-start | bytes 1179652
  80.7 95.1 %all-to-all-start = ((bf16[4,64,768]{2,1,0:T(8,128)(2,1)}), bf16[4,64,768]{2,1,0:T(8,128)(2,1)S(1)}, u32[]{:S(2)}, u32[]{:S(2)}) async-start(bf16[4,64,768]{2,1,0:T(8,128)(2,1)} %get-tuple-element.117), calls=%async_computation | async-start | bytes 786432 | tf_op jit(solution)/shard_map/all_to_all | solution.py:255
  155.4 38.8 %copy-start.21 = (bf16[256,2304]{0,1:T(8,128)(2,1)}, bf16[256,2304]{0,1:T(8,128)(2,1)S(1)}, u32[]{:S(2)}) copy-start(bf16[256,2304]{0,1:T(8,128)(2,1)S(1)} %copy.364) | copy-start | bytes 3538948
  175.8 8.9 copy-start.68
  175.8 21.0 %all-to-all-start.4 = ((bf16[2,128,3,768]{1,0,2,3:T(2,128)(2,1)}), bf16[2,128,3,768]{1,0,2,3:T(2,128)(2,1)}, u32[]{:S(2)}, u32[]{:S(2)}) async-start(bf16[2,128,3,768]{1,0,2,3:T(2,128)(2,1)} %copy.368), calls=%async_computation.4 | async-start | bytes 2359296 | tf_op jit(solution)/shard_map/all_to_all | solution.py:70
  196.7 9.7 copy-start.93
  196.9 19.5 %all-to-all-start.6 = ((bf16[2,128,3,768]{1,0,2,3:T(2,128)(2,1)}), bf16[2,128,3,768]{1,0,2,3:T(2,128)(2,1)S(1)}, u32[]{:S(2)}, u32[]{:S(2)}) async-start(bf16[2,128,3,768]{1,0,2,3:T(2,128)(2,1)} %copy.375), calls=%async_computation.6 | async-start | bytes 2359296 | tf_op jit(solution)/shard_map/all_to_all | solution.py:70
  209.6 11.4 %copy-start.82 = (pred[2,512]{1,0:T(4,128)(4,1)S(1)}, pred[2,512]{1,0:T(4,128)(4,1)}, u32[]{:S(2)}) copy-start(pred[2,512]{1,0:T(4,128)(4,1)} %get-tuple-element.209) | copy-start | bytes 3076
  230.8 14.6 %all-to-all-start.7 = ((bf16[2,512,192]{2,0,1:T(2,128)(2,1)}), bf16[2,512,192]{2,0,1:T(2,128)(2,1)S(1)}, u32[]{:S(2)}, u32[]{:S(2)}) async-start(bf16[2,512,192]{2,0,1:T(2,128)(2,1)} %copy.379), calls=%async_computation.7 | async-start | bytes 1048576 | tf_op jit(solution)/shard_map/all_to_all | solution.py:92
  244.3 15.8 %copy-start.129 = (f32[768]{0:T(1024)S(1)}, f32[768]{0:T(1024)}, u32[]{:S(2)}) copy-start(f32[768]{0:T(1024)} %get-tuple-element.58) | copy-start | bytes 9220
  245.4 12.5 %all-to-all-start.5 = ((bf16[2,512,192]{2,0,1:T(2,128)(2,1)}), bf16[2,512,192]{2,0,1:T(2,128)(2,1)S(1)}, u32[]{:S(2)}, u32[]{:S(2)}) async-start(bf16[2,512,192]{2,0,1:T(2,128)(2,1)} %copy.372), calls=%async_computation.5 | async-start | bytes 1048576 | tf_op jit(solution)/shard_map/all_to_all | solution.py:92
  264.2 13.5 %copy-start.32 = (f32[256,768]{1,0:T(8,128)}, f32[256,768]{1,0:T(8,128)S(1)}, u32[]{:S(2)}) copy-start(f32[256,768]{1,0:T(8,128)S(1)} %get-tuple-element.170) | copy-start | bytes 2359300
  277.7 14.3 %slice-start.3 = ((s8[4718592]{0:T(1024)(128)(4,1)}), s8[4194304]{0:T(1024)(128)(4,1)S(1)}, s32[]{:S(2)}) async-start(s8[4718592]{0:T(1024)(128)(4,1)} %bitcast.462), calls=%async_computation.32 | async-start | bytes 8388608
  277.7 17.1 %slice-start = ((s8[9437184]{0:T(1024)(128)(4,1)}), s8[4194304]{0:T(1024)(128)(4,1)S(1)}, s32[]{:S(2)}) async-start(s8[9437184]{0:T(1024)(128)(4,1)} %bitcast.460), calls=%async_computation.29 | async-start | bytes 8388608
  282.5 9.6 copy-start.96
  282.5 9.6 copy-start.112
  282.5 9.6 copy-start.127
  282.5 9.6 slice-start.4
  282.5 12.3 %slice-start.1 = ((s8[9437184]{0:T(1024)(128)(4,1)}), s8[4194304]{0:T(1024)(128)(4,1)S(1)}, s32[]{:S(2)}) async-start(s8[9437184]{0:T(1024)(128)(4,1)} %bitcast.460), calls=%async_computation.30 | async-start | bytes 8388608
  282.6 12.3 %slice-start.2 = ((s8[9437184]{0:T(1024)(128)(4,1)}), s8[1048576]{0:T(1024)(128)(4,1)S(1)}, s32[]{:S(2)}) async-start(s8[9437184]{0:T(1024)(128)(4,1)} %bitcast.460), calls=%async_computation.31 | async-start | bytes 2097152
  294.9 10.0 copy-start.114
  306.7 9.7 copy-start.110
  322.2 17.7 %copy-start.61 = (bf16[256,768]{1,0:T(8,128)(2,1)}, bf16[256,768]{1,0:T(8,128)(2,1)S(1)}, u32[]{:S(2)}) copy-start(bf16[256,768]{1,0:T(8,128)(2,1)S(1)} %get-tuple-element.100) | copy-start | bytes 1179652
  324.4 10.9 copy-start.63
  354.6 9.3 copy-start.52
  359.8 33.5 %all-to-all-start.14 = ((bf16[2,128,768]{1,0,2:T(2,128)(2,1)}), bf16[2,128,768]{1,0,2:T(2,128)(2,1)}, u32[]{:S(2)}, u32[]{:S(2)}) async-start(bf16[2,128,768]{1,0,2:T(2,128)(2,1)} %copy.403), calls=%async_computation.14 | async-start | bytes 786432 | tf_op jit(solution)/shard_map/all_to_all | solution.py:137
  363.9 325.7 %reduce-scatter.10.cloned.1.call-start = ((), (), s32[]{:S(2)}) async-start(), calls=%async_computation.24 | async-start | bytes 2654208 | tf_op jit(solution)/shard_map/reduce_scatter | solution.py:280
  390.1 11.4 %copy-start.5 = (bf16[2,3,512,512]{2,3,1,0:T(8,128)(2,1)S(1)}, bf16[2,3,512,512]{2,3,1,0:T(8,128)(2,1)}, u32[]{:S(2)}) copy-start(bf16[2,3,512,512]{2,3,1,0:T(8,128)(2,1)} %copy-done.4) | copy-start | bytes 9437188
  393.3 13.1 %all-to-all-start.12 = ((bf16[2,128,768]{1,0,2:T(2,128)(2,1)}), bf16[2,128,768]{1,0,2:T(2,128)(2,1)}, u32[]{:S(2)}, u32[]{:S(2)}) async-start(bf16[2,128,768]{1,0,2:T(2,128)(2,1)} %copy.391), calls=%async_computation.12 | async-start | bytes 786432 | tf_op jit(solution)/shard_map/all_to_all | solution.py:137
  447.3 38.1 %all-to-all-start.13 = ((bf16[2,512,3,192]{3,0,2,1:T(2,128)(2,1)}), bf16[2,512,3,192]{3,0,2,1:T(2,128)(2,1)S(1)}, u32[]{:S(2)}, u32[]{:S(2)}) async-start(bf16[2,512,3,192]{3,0,2,1:T(2,128)(2,1)} %pad_maximum_fusion), calls=%async_computation.13 | async-start | bytes 3145728 | tf_op jit(solution)/shard_map/all_to_all | solution.py:169
  480.6 9.3 copy-start.20
  485.5 29.6 %all-to-all-start.15 = ((bf16[2,512,3,192]{3,0,2,1:T(2,128)(2,1)}), bf16[2,512,3,192]{3,0,2,1:T(2,128)(2,1)}, u32[]{:S(2)}, u32[]{:S(2)}) async-start(bf16[2,512,3,192]{3,0,2,1:T(2,128)(2,1)} %pad_maximum_fusion.1), calls=%async_computation.15 | async-start | bytes 3145728 | tf_op jit(solution)/shard_map/all_to_all | solution.py:169
  489.9 201.4 %reduce-scatter.8.cloned.1.call-start = ((), (), s32[]{:S(2)}) async-start(), calls=%async_computation.23 | async-start | bytes 7962624 | tf_op jit(solution)/shard_map/reduce_scatter | solution.py:279
  528.7 294.7 %reduce-scatter.12.cloned.1.call-start = ((), (), s32[]{:S(2)}) async-start(), calls=%async_computation.25 | async-start | bytes 10616832 | tf_op jit(solution)/shard_map/reduce_scatter | solution.py:281
  538.7 451.2 %reduce-scatter.14.cloned.1.call-start = ((), (), s32[]{:S(2)}) async-start(), calls=%async_computation.26 | async-start | bytes 10616832 | tf_op jit(solution)/shard_map/reduce_scatter | solution.py:282
  549.1 13.8 %copy-start.98 = (f32[768]{0:T(1024)S(1)}, f32[768]{0:T(1024)}, u32[]{:S(2)}) copy-start(f32[768]{0:T(1024)} %get-tuple-element.43) | copy-start | bytes 9220
  549.1 14.3 %copy-start.97 = (f32[768]{0:T(1024)S(1)}, f32[768]{0:T(1024)}, u32[]{:S(2)}) copy-start(f32[768]{0:T(1024)} %get-tuple-element.44) | copy-start | bytes 9220
  549.1 14.9 %copy-start.100 = (f32[768]{0:T(1024)S(1)}, f32[768]{0:T(1024)}, u32[]{:S(2)}) copy-start(f32[768]{0:T(1024)} %get-tuple-element.51) | copy-start | bytes 9220
  549.1 15.5 %copy-start.99 = (f32[768]{0:T(1024)S(1)}, f32[768]{0:T(1024)}, u32[]{:S(2)}) copy-start(f32[768]{0:T(1024)} %get-tuple-element.156) | copy-start | bytes 9220
  558.7 48.9 %all-to-all-start.3 = ((bf16[4,2,24576]{2,1,0:T(2,128)(2,1)}), bf16[4,2,24576]{2,1,0:T(2,128)(2,1)}, u32[]{:S(2)}, u32[]{:S(2)}) async-start(bf16[4,2,24576]{2,1,0:T(2,128)(2,1)} %reshape.971), calls=%async_computation.3 | async-start | bytes 786432 | tf_op jit(solution)/shard_map/all_to_all | solution.py:265
  564.6 23.2 %copy-start.101 = (f32[768]{0:T(1024)S(1)}, f32[768]{0:T(1024)}, u32[]{:S(2)}) copy-start(f32[768]{0:T(1024)} %get-tuple-element.108) | copy-start | bytes 9220
  607.6 16.1 %all-to-all-start.1 = ((bf16[4,2,24576]{2,1,0:T(2,128)(2,1)}), bf16[4,2,24576]{2,1,0:T(2,128)(2,1)}, u32[]{:S(2)}, u32[]{:S(2)}) async-start(bf16[4,2,24576]{2,1,0:T(2,128)(2,1)} %reshape.973), calls=%async_computation.1 | async-start | bytes 786432 | tf_op jit(solution)/shard_map/all_to_all | solution.py:265
  623.6 15.8 %all-to-all-start.11 = ((bf16[4,2,24576]{2,1,0:T(2,128)(2,1)}), bf16[4,2,24576]{2,1,0:T(2,128)(2,1)}, u32[]{:S(2)}, u32[]{:S(2)}) async-start(bf16[4,2,24576]{2,1,0:T(2,128)(2,1)} %reshape.975), calls=%async_computation.11 | async-start | bytes 786432 | tf_op jit(solution)/shard_map/all_to_all | solution.py:266
  631.4 18.9 %copy-start.106 = (f32[768,1]{0,1:T(1,128)S(1)}, f32[768,1]{0,1:T(1,128)}, u32[]{:S(2)}) copy-start(f32[768,1]{0,1:T(1,128)} %stack.187) | copy-start | bytes 9220
  639.5 31.4 %all-to-all-start.9 = ((bf16[4,2,24576]{2,1,0:T(2,128)(2,1)}), bf16[4,2,24576]{2,1,0:T(2,128)(2,1)}, u32[]{:S(2)}, u32[]{:S(2)}) async-start(bf16[4,2,24576]{2,1,0:T(2,128)(2,1)} %reshape.977), calls=%async_computation.9 | async-start | bytes 786432 | tf_op jit(solution)/shard_map/all_to_all | solution.py:266
  643.6 411.0 %reduce-scatter.16.cloned.1.call-start = ((), (), s32[]{:S(2)}) async-start(), calls=%async_computation.27 | async-start | bytes 442368
  684.8 420.0 %all-reduce.3.cloned.1.call-start = ((), (), s32[]{:S(2)}) async-start(), calls=%async_computation.28 | async-start | bytes 3538944 | tf_op jit(solution)/shard_map/psum | solution.py:288
  992.1 69.1 %copy-start.90 = (f32[96,12]{0,1:T(8,128)S(1)}, f32[96,12]{0,1:T(8,128)}, u32[]{:S(2)}) copy-start(f32[96,12]{0,1:T(8,128)} %param.23) | copy-start | bytes 13828
  992.1 70.4 %copy-start.119 = (f32[96,12]{0,1:T(8,128)S(1)}, f32[96,12]{0,1:T(8,128)}, u32[]{:S(2)}) copy-start(f32[96,12]{0,1:T(8,128)} %param.29) | copy-start | bytes 13828
  992.1 112.7 %copy-start.29 = (f32[384,768]{1,0:T(8,128)S(1)}, f32[384,768]{1,0:T(8,128)}, u32[]{:S(2)}) copy-start(f32[384,768]{1,0:T(8,128)} %param.22) | copy-start | bytes 3538948
  992.1 112.7 %copy-start.38 = (f32[384,768]{1,0:T(8,128)S(1)}, f32[384,768]{1,0:T(8,128)}, u32[]{:S(2)}) copy-start(f32[384,768]{1,0:T(8,128)} %param.25) | copy-start | bytes 3538948
  1062.5 45.5 %copy-start.88 = (f32[96,12]{0,1:T(8,128)}, f32[96,12]{0,1:T(8,128)S(1)}, u32[]{:S(2)}) copy-start(f32[96,12]{0,1:T(8,128)S(1)} %get-tuple-element.66) | copy-start | bytes 13828
  (111 other events, 379.1 us)
Sparse Core Ops, SparseCore 0:
  10.8 140.8 all-gather.3
  154.4 78.0 all-gather.5
  376.8 67.9 reduce-scatter.9
  528.9 128.0 reduce-scatter.7
  660.9 162.5 reduce-scatter.11
  827.3 162.5 reduce-scatter.13
  994.1 60.5 reduce-scatter.15
  1059.1 45.6 all-reduce.2
where the time goes:
time: 1130 us; the launch traced here: 1120 us
  waiting for transfers between devices  485 us (43%)
  matrix products  251 us (22%)
  local copies, waits for them, and re-layouts  169 us (15%)
  other arithmetic  99.7 us (9%)
  starting transfers between devices  64.3 us (6%)
  blocking collectives  38 us (3%)
  between operations  16.8 us (1%)
    reduce_scatter x1, waiting for transfers between devices, body(): lax.psum_scatter(products[3], 'dp', scatter_dimension=0, tiled=True)  164 us
    reduce_scatter x1, waiting for transfers between devices, body(): lax.psum_scatter(products[2], 'dp', scatter_dimension=0, tiled=True)  130 us
    all_gather x1, waiting for transfers between devices, body(): lax.all_gather(wide_master.astype(jnp.bfloat16), 'dp', axis=0, tiled=True)  67.5 us
    unnamed x9, waiting for transfers between devices  58.2 us
    unnamed x321, local copies, waits for them, and re-layouts  49 us
    dot_general x16, matrix products, right_dot(): jnp.einsum('ra,ba->rb', left, right, preferred_element_type=jnp.float32)  44.5 us
    psum x1, waiting for transfers between devices, body(): lax.psum(sums[2].astype(jnp.bfloat16), 'seq').astype(jnp.float32)  41.8 us
    dot_general x4, matrix products, micro_step(): jnp.dot(first_low, wide_w[:, 4 * model_width:], preferred_element_type=jn...  39.9 us
  transfers between devices with their start and end apart: 24, of which 9 were waited for; matrix products, arithmetic and copies ran while one was open for 37% of the time, Pallas kernels for 0%

commit v1 on v0

--- a/solution.py
+++ b/solution.py
@@ -12,6 +12,28 @@
 momentum_rate = 0.9
 decay_weight = 0.0001
 average_rate = 0.9
+
+
+def in_order(parts, dim):
+    parts = jnp.moveaxis(parts, 0, dim)
+    shape = parts.shape
+    return parts.reshape(*shape[:dim], shape[dim] * shape[dim + 1], *shape[dim + 2 :])
+
+
+def grow_blocks(x, axis):
+    count = lax.axis_size(axis)
+    parts = x[None]
+    for level in range(count.bit_length() - 1):
+        distance = 1 << level
+        partner_block = lax.ppermute(parts, axis, [(i, i ^ distance) for i in range(count)])
+        both = jnp.stack([parts, partner_block])
+        upper = lax.axis_index(axis) >> level & 1
+        parts = jnp.where(upper == 0, both, both[::-1]).reshape(-1, *x.shape)
+    return parts
+
+
+def collect(x, axis, dim):
+    return in_order(grow_blocks(x, axis), dim)
 
 
 def norm_forward(inputs, gain, shift):
@@ -227,7 +249,7 @@
     weights = (
         lax.all_gather(wide_master.astype(jnp.bfloat16), "dp", axis=0, tiled=True),
         lax.all_gather(down_master.astype(jnp.bfloat16), "dp", axis=0, tiled=True),
-        lax.all_gather(vector_master.astype(jnp.bfloat16), "dp", axis=0, tiled=True),
+        collect(vector_master.astype(jnp.bfloat16), "dp", 0),
     )
     own_rows = wide_master.shape[0]
     sums = (

time: 1130 us -> 1130 us (level)
  blocking collectives: 38 us -> 5.67 us
  waiting for transfers between devices: 485 us -> 510 us
    all_gather x1 -> x0, blocking collectives: 32.3 us -> none  [body(): lax.all_gather(vector_master.astype(jnp.bfloat16), 'dp', axis=0, tiled=True)]
    all_gather x1, waiting for transfers between devices: 67.5 us -> 88.1 us  [body(): lax.all_gather(wide_master.astype(jnp.bfloat16), 'dp', axis=0, tiled=True)]
    unnamed x321 -> x319, local copies, waits for them, and re-layouts: 49 us -> 49.1 us
  transfers between devices with their start and end apart: 24 -> 27, of which waited for: 9 -> 11; matrix products, arithmetic and copies ran while one was open for 37% -> 37% of each run, Pallas kernels for 0% -> 0%
where the time goes in v1:
time: 1130 us; the launch traced here: 1120 us
  waiting for transfers between devices  510 us (45%)
  matrix products  251 us (22%)
  local copies, waits for them, and re-layouts  170 us (15%)
  other arithmetic  99.7 us (9%)
  starting transfers between devices  70.7 us (6%)
  between operations  16.9 us (1%)
    reduce_scatter x1, waiting for transfers between devices, body(): lax.psum_scatter(products[3], 'dp', scatter_dimension=0, tiled=True)  164 us
    reduce_scatter x1, waiting for transfers between devices, body(): lax.psum_scatter(products[2], 'dp', scatter_dimension=0, tiled=True)  130 us
    all_gather x1, waiting for transfers between devices, body(): lax.all_gather(wide_master.astype(jnp.bfloat16), 'dp', axis=0, tiled=True)  88.1 us
    unnamed x9, waiting for transfers between devices  58.2 us
    unnamed x319, local copies, waits for them, and re-layouts  49.1 us
    dot_general x16, matrix products, right_dot(): jnp.einsum('ra,ba->rb', left, right, preferred_element_type=jnp.float32)  44.5 us
    psum x1, waiting for transfers between devices, body(): lax.psum(sums[2].astype(jnp.bfloat16), 'seq').astype(jnp.float32)  41.7 us
    dot_general x4, matrix products, micro_step(): jnp.dot(first_low, wide_w[:, 4 * model_width:], preferred_element_type=jn...  39.9 us
  transfers between devices with their start and end apart: 27, of which 11 were waited for; matrix products, arithmetic and copies ran while one was open for 37% of the time, Pallas kernels for 0%

profile of v1, /device:TPU:0, one launch (start us, length us, event | category | flops | bytes accessed | tf_op | source)
XLA Modules:
  0.0 1123.7 jit_solution(11011115772584980856)
XLA Ops:
  14.2 3.5 all-to-all-start.8
  38.7 3.5 all-to-all-start.10
  42.7 6.8 all-to-all-done.10
  49.5 3.5 all-to-all-start.2
  55.2 5.2 all-to-all-done.2
  60.4 3.5 all-to-all-start
  63.9 88.1 %all-gather.3.cloned.1.call-done = bf16[768,6144]{1,0:T(8,128)(2,1)} async-done(((bf16[96,6144]{1,0:T(8,128)(2,1)}), bf16[768,6144]{1,0:T(8,128)(2,1)}) %all-gather.3.cloned.1.call-update) | async-done | bytes 9437200 | tf_op jit(solution)/shard_map/all_gather | solution.py:250
  155.8 3.6 fusion.42
  161.3 5.0 copy.375
  171.2 5.0 copy.382
  176.2 4.8 all-to-all-start.4
  181.0 4.1 fusion.40
  197.3 3.7 all-to-all-start.6
  209.9 6.9 all-to-all-done.6
  231.2 3.5 all-to-all-start.7
  245.8 3.7 all-to-all-start.5
  252.1 6.2 all-to-all-done.5
  267.3 10.8 fusion.66
  278.1 4.5 fusion.385
  282.9 9.5 fusion.63
  295.3 10.0 fusion.69
  307.1 9.6 fusion.60
  344.2 3.6 convert_reduce_fusion.11
  360.2 4.1 all-to-all-start.14
  373.0 4.0 fusion.177
  377.1 6.7 fusion.241
  383.7 6.7 fusion.247
  393.7 4.1 all-to-all-start.12
  414.9 5.0 fusion.316
  419.9 11.7 %fusion.269 = bf16[2,3,64,512]{3,2,1,0:T(8,128)(2,1)S(1)} fusion(f32[2,3,512,512]{2,3,1,0:T(8,128)} %fusion.316, f32[2,3,512,512]{2,3,1,0:T(8,128)} %copy-done.1, f32[2,3,512]{2,1,0:T(4,128)S(1)} %copy-done.103, pred[2,512]{1,0:T(4,128)(4,1)S(1)} %copy-done.84, bf16[2,512,3,3,64]{1,4,3,0,2:T(8,128)(2,1)S(1)} %copy-done.18), kind=kOutput, calls=%fused_computation.309 | convolution fusion | flops 219024896 | bytes 25989120 | tf_op jit(solution)/shard_map/bhqk,bkhd->bqhd/dot_general | solution.py:178
  432.1 11.9 %fusion.266 = bf16[2,3,64,512]{3,2,1,0:T(8,128)(2,1)S(1)} fusion(f32[2,3,512,512]{2,3,1,0:T(8,128)} %fusion.316, f32[2,3,512,512]{2,3,1,0:T(8,128)} %copy-done.1, f32[2,3,512]{2,1,0:T(4,128)S(1)} %copy-done.103, pred[2,512]{1,0:T(4,128)(4,1)S(1)} %copy-done.84, bf16[2,512,3,3,64]{1,4,3,0,2:T(8,128)(2,1)S(1)} %copy-done.18), kind=kOutput, calls=%fused_computation.308 | convolution fusion | flops 219024896 | bytes 25989120 | tf_op jit(solution)/shard_map/bhqk,bqhd->bkhd/dot_general | solution.py:182
  447.7 4.0 all-to-all-start.13
  451.7 3.7 fusion.318
  455.4 11.6 %fusion.275 = bf16[2,3,64,512]{3,2,1,0:T(8,128)(2,1)S(1)} fusion(f32[2,3,512,512]{2,3,1,0:T(8,128)} %fusion.318, f32[2,3,512,512]{2,3,1,0:T(8,128)} %copy-done, f32[2,3,512]{2,1,0:T(4,128)} %log_add_fusion, pred[2,512]{1,0:T(4,128)(4,1)S(1)} %copy-done.82, bf16[2,512,3,3,64]{1,4,3,0,2:T(8,128)(2,1)S(1)} %copy-done.17), kind=kOutput, calls=%fused_computation.311 | convolution fusion | flops 219024896 | bytes 25989120 | tf_op jit(solution)/shard_map/bhqk,bkhd->bqhd/dot_general | solution.py:178
  468.1 11.8 %fusion.272 = bf16[2,3,64,512]{3,2,1,0:T(8,128)(2,1)S(1)} fusion(f32[2,3,512,512]{2,3,1,0:T(8,128)} %fusion.318, f32[2,3,512,512]{2,3,1,0:T(8,128)} %copy-done, f32[2,3,512]{2,1,0:T(4,128)} %log_add_fusion, pred[2,512]{1,0:T(4,128)(4,1)S(1)} %copy-done.82, bf16[2,512,3,3,64]{1,4,3,0,2:T(8,128)(2,1)S(1)} %copy-done.17), kind=kOutput, calls=%fused_computation.310 | convolution fusion | flops 219024896 | bytes 25989120 | tf_op jit(solution)/shard_map/bhqk,bqhd->bkhd/dot_general | solution.py:182
  481.0 4.9 pad_maximum_fusion.1
  485.9 4.4 all-to-all-start.15
  492.6 6.9 fusion.253
  499.5 6.9 fusion.259
  515.4 3.6 copy.420
  521.4 7.7 fusion.28
  529.2 9.9 fusion.4
  539.1 10.3 fusion.12
  552.5 4.7 reduce.54
  559.1 4.1 all-to-all-start.3
  578.3 4.7 reduce.55
  608.0 4.4 all-to-all-start.1
  612.3 3.7 fusion.282
  617.5 4.7 reduce.56
  624.0 4.1 all-to-all-start.11
  628.1 3.7 fusion.283
  633.3 4.7 reduce.57
  639.8 4.1 all-to-all-start.9
  655.5 3.3 reshape.980
  666.0 3.3 reshape.984
  671.3 3.3 reshape.986
  685.6 4.4 fusion.280
  693.6 130.0 %reduce-scatter.12.cloned.1.call-done = f32[96,3072]{1,0:T(8,128)} async-done(((f32[768,3072]{1,0:T(8,128)}), f32[96,3072]{1,0:T(8,128)}) %reduce-scatter.12.cloned.1.call-update) | async-done | bytes 1179664 | tf_op jit(solution)/shard_map/reduce_scatter | solution.py:303
  825.8 164.3 %reduce-scatter.14.cloned.1.call-done = f32[384,768]{1,0:T(8,128)} async-done(((f32[3072,768]{1,0:T(8,128)}), f32[384,768]{1,0:T(8,128)}) %reduce-scatter.14.cloned.1.call-update) | async-done | bytes 1179664 | tf_op jit(solution)/shard_map/reduce_scatter | solution.py:304
  992.3 3.5 fusion.281
  996.7 58.0 %reduce-scatter.16.cloned.1.call-done = f32[96,12]{1,0:T(8,128)} async-done(((f32[768,12]{1,0:T(8,128)}), f32[96,12]{1,0:T(8,128)}) %reduce-scatter.16.cloned.1.call-update) | async-done | bytes 4624
  1055.6 5.7 psum.39
  1063.2 41.7 %all-reduce.3.cloned.1.call-done = (bf16[96,3072]{1,0:T(8,128)(2,1)}, bf16[96,768]{1,0:T(8,128)(2,1)}, bf16[96,2304]{1,0:T(8,128)(2,1)}, bf16[384,768]{1,0:T(8,128)(2,1)}) async-done(((bf16[96,3072]{1,0:T(8,128)(2,1)}, bf16[96,768]{1,0:T(8,128)(2,1)}, bf16[96,2304]{1,0:T(8,128)(2,1)}, bf16[384,768]{1,0:T(8,128)(2,1)}), (bf16[96,3072]{1,0:T(8,128)(2,1)}, bf16[96,768]{1,0:T(8,128)(2,1)}, ...) | async-done | bytes 1769488 | tf_op jit(solution)/shard_map/psum | solution.py:310
  1110.9 3.4 fusion.369
  (582 shorter events, 294.9 us)
Async XLA Ops:
  7.2 10.5 copy-start.28
  7.2 144.8 %all-gather.3.cloned.1.call-start = ((), (), s32[]{:S(2)}) async-start(), calls=%async_computation.21 | async-start | bytes 10616832 | tf_op jit(solution)/shard_map/all_gather | solution.py:250
  10.2 11.0 copy-start.131
  10.2 13.0 %copy-start.44 = (bf16[2,4,64,768]{3,2,1,0:T(8,128)(2,1)S(1)}, bf16[2,4,64,768]{3,2,1,0:T(8,128)(2,1)}, u32[]{:S(2)}) copy-start(bf16[2,4,64,768]{3,2,1,0:T(8,128)(2,1)} %param.15) | copy-start | bytes 2359300
  10.3 17.2 %collective-permute-start = (bf16[1,96,12]{1,2,0:T(8,128)(2,1)S(1)}, bf16[1,96,12]{1,2,0:T(8,128)(2,1)S(1)}, u32[]{:S(2)}, u32[]{:S(2)}) collective-permute-start(bf16[1,96,12]{1,2,0:T(8,128)(2,1)S(1)} %get-tuple-element.138), channel_id=1, source_target_pairs={{0,4},{4,0},{8,12},{12,8},{16,20},{20,16},{24,28},{28,24},{1,5},{5... | collective-permute-start | bytes 6920 | tf_op jit(solution)/shard_map/ppermute | solution.py:28
  14.2 24.4 %all-to-all-start.8 = ((bf16[4,64,768]{2,1,0:T(8,128)(2,1)}), bf16[4,64,768]{2,1,0:T(8,128)(2,1)S(1)}, u32[]{:S(2)}, u32[]{:S(2)}) async-start(bf16[4,64,768]{2,1,0:T(8,128)(2,1)} %get-tuple-element.113), calls=%async_computation.8 | async-start | bytes 786432 | tf_op jit(solution)/shard_map/all_to_all | solution.py:278
  17.7 20.1 %copy-start.14 = (bf16[2,2,128,768]{3,2,1,0:T(8,128)(2,1)S(1)}, bf16[2,2,128,768]{3,2,1,0:T(8,128)(2,1)}, u32[]{:S(2)}) copy-start(bf16[2,2,128,768]{3,2,1,0:T(8,128)(2,1)} %param.18) | copy-start | bytes 2359300
  17.7 260.4 %all-gather.5.cloned.1.call-start = ((), (), s32[]{:S(2)}) async-start(), calls=%async_computation.22 | async-start | bytes 5308416 | tf_op jit(solution)/shard_map/all_gather | solution.py:251
  27.4 3.9 collective-permute-start.1
  31.4 5.0 collective-permute-start.2
  37.7 114.3 %copy-start.74 = (f32[768]{0:T(1024)}, f32[768]{0:T(1024)S(1)}, u32[]{:S(2)}) copy-start(f32[768]{0:T(1024)S(1)} %get-tuple-element.53) | copy-start | bytes 9220
  38.7 113.4 %copy-start.25 = (bf16[4,64,768]{2,1,0:T(8,128)(2,1)}, bf16[4,64,768]{2,1,0:T(8,128)(2,1)S(1)}, u32[]{:S(2)}) copy-start(bf16[4,64,768]{2,1,0:T(8,128)(2,1)S(1)} %all-to-all-done.8) | copy-start | bytes 1179652
  38.7 10.9 all-to-all-start.10
  49.5 10.9 all-to-all-start.2
  60.4 94.7 %copy-start.64 = (bf16[4,64,768]{2,1,0:T(8,128)(2,1)}, bf16[4,64,768]{2,1,0:T(8,128)(2,1)S(1)}, u32[]{:S(2)}) copy-start(bf16[4,64,768]{2,1,0:T(8,128)(2,1)S(1)} %all-to-all-done.2) | copy-start | bytes 1179652
  60.4 115.8 %all-to-all-start = ((bf16[4,64,768]{2,1,0:T(8,128)(2,1)}), bf16[4,64,768]{2,1,0:T(8,128)(2,1)S(1)}, u32[]{:S(2)}, u32[]{:S(2)}) async-start(bf16[4,64,768]{2,1,0:T(8,128)(2,1)} %get-tuple-element.117), calls=%async_computation | async-start | bytes 786432 | tf_op jit(solution)/shard_map/all_to_all | solution.py:277
  155.7 38.8 %copy-start.21 = (bf16[256,2304]{0,1:T(8,128)(2,1)}, bf16[256,2304]{0,1:T(8,128)(2,1)S(1)}, u32[]{:S(2)}) copy-start(bf16[256,2304]{0,1:T(8,128)(2,1)S(1)} %copy.371) | copy-start | bytes 3538948
  176.2 21.0 %all-to-all-start.4 = ((bf16[2,128,3,768]{1,0,2,3:T(2,128)(2,1)}), bf16[2,128,3,768]{1,0,2,3:T(2,128)(2,1)}, u32[]{:S(2)}, u32[]{:S(2)}) async-start(bf16[2,128,3,768]{1,0,2,3:T(2,128)(2,1)} %copy.375), calls=%async_computation.4 | async-start | bytes 2359296 | tf_op jit(solution)/shard_map/all_to_all | solution.py:92
  197.0 9.7 copy-start.92
  197.3 19.5 %all-to-all-start.6 = ((bf16[2,128,3,768]{1,0,2,3:T(2,128)(2,1)}), bf16[2,128,3,768]{1,0,2,3:T(2,128)(2,1)S(1)}, u32[]{:S(2)}, u32[]{:S(2)}) async-start(bf16[2,128,3,768]{1,0,2,3:T(2,128)(2,1)} %copy.382), calls=%async_computation.6 | async-start | bytes 2359296 | tf_op jit(solution)/shard_map/all_to_all | solution.py:92
  209.9 11.5 %copy-start.81 = (pred[2,512]{1,0:T(4,128)(4,1)S(1)}, pred[2,512]{1,0:T(4,128)(4,1)}, u32[]{:S(2)}) copy-start(pred[2,512]{1,0:T(4,128)(4,1)} %get-tuple-element.213) | copy-start | bytes 3076
  231.2 14.6 %all-to-all-start.7 = ((bf16[2,512,192]{2,0,1:T(2,128)(2,1)}), bf16[2,512,192]{2,0,1:T(2,128)(2,1)S(1)}, u32[]{:S(2)}, u32[]{:S(2)}) async-start(bf16[2,512,192]{2,0,1:T(2,128)(2,1)} %copy.386), calls=%async_computation.7 | async-start | bytes 1048576 | tf_op jit(solution)/shard_map/all_to_all | solution.py:114
  244.7 15.8 %copy-start.128 = (f32[768]{0:T(1024)S(1)}, f32[768]{0:T(1024)}, u32[]{:S(2)}) copy-start(f32[768]{0:T(1024)} %get-tuple-element.58) | copy-start | bytes 9220
  245.8 12.5 %all-to-all-start.5 = ((bf16[2,512,192]{2,0,1:T(2,128)(2,1)}), bf16[2,512,192]{2,0,1:T(2,128)(2,1)S(1)}, u32[]{:S(2)}, u32[]{:S(2)}) async-start(bf16[2,512,192]{2,0,1:T(2,128)(2,1)} %copy.379), calls=%async_computation.5 | async-start | bytes 1048576 | tf_op jit(solution)/shard_map/all_to_all | solution.py:114
  264.6 13.5 %copy-start.32 = (f32[256,768]{1,0:T(8,128)}, f32[256,768]{1,0:T(8,128)S(1)}, u32[]{:S(2)}) copy-start(f32[256,768]{1,0:T(8,128)S(1)} %get-tuple-element.174) | copy-start | bytes 2359300
  278.1 14.3 %slice-start.3 = ((s8[4718592]{0:T(1024)(128)(4,1)}), s8[4194304]{0:T(1024)(128)(4,1)S(1)}, s32[]{:S(2)}) async-start(s8[4718592]{0:T(1024)(128)(4,1)} %bitcast.478), calls=%async_computation.32 | async-start | bytes 8388608
  278.1 17.1 %slice-start = ((s8[9437184]{0:T(1024)(128)(4,1)}), s8[4194304]{0:T(1024)(128)(4,1)S(1)}, s32[]{:S(2)}) async-start(s8[9437184]{0:T(1024)(128)(4,1)} %bitcast.476), calls=%async_computation.29 | async-start | bytes 8388608
  282.9 9.6 copy-start.95
  282.9 9.6 copy-start.111
  282.9 9.6 copy-start.126
  282.9 9.6 slice-start.4
  282.9 12.3 %slice-start.1 = ((s8[9437184]{0:T(1024)(128)(4,1)}), s8[4194304]{0:T(1024)(128)(4,1)S(1)}, s32[]{:S(2)}) async-start(s8[9437184]{0:T(1024)(128)(4,1)} %bitcast.476), calls=%async_computation.30 | async-start | bytes 8388608
  282.9 12.3 %slice-start.2 = ((s8[9437184]{0:T(1024)(128)(4,1)}), s8[1048576]{0:T(1024)(128)(4,1)S(1)}, s32[]{:S(2)}) async-start(s8[9437184]{0:T(1024)(128)(4,1)} %bitcast.476), calls=%async_computation.31 | async-start | bytes 2097152
  295.3 10.0 copy-start.113
  307.1 9.7 copy-start.109
  322.5 17.7 %copy-start.60 = (bf16[256,768]{1,0:T(8,128)(2,1)}, bf16[256,768]{1,0:T(8,128)(2,1)S(1)}, u32[]{:S(2)}) copy-start(bf16[256,768]{1,0:T(8,128)(2,1)S(1)} %get-tuple-element.100) | copy-start | bytes 1179652
  324.8 10.9 copy-start.62
  360.2 33.5 %all-to-all-start.14 = ((bf16[2,128,768]{1,0,2:T(2,128)(2,1)}), bf16[2,128,768]{1,0,2:T(2,128)(2,1)}, u32[]{:S(2)}, u32[]{:S(2)}) async-start(bf16[2,128,768]{1,0,2:T(2,128)(2,1)} %copy.410), calls=%async_computation.14 | async-start | bytes 786432 | tf_op jit(solution)/shard_map/all_to_all | solution.py:159
  364.3 325.7 %reduce-scatter.10.cloned.1.call-start = ((), (), s32[]{:S(2)}) async-start(), calls=%async_computation.24 | async-start | bytes 2654208 | tf_op jit(solution)/shard_map/reduce_scatter | solution.py:302
  390.5 11.4 %copy-start.5 = (bf16[2,3,512,512]{2,3,1,0:T(8,128)(2,1)S(1)}, bf16[2,3,512,512]{2,3,1,0:T(8,128)(2,1)}, u32[]{:S(2)}) copy-start(bf16[2,3,512,512]{2,3,1,0:T(8,128)(2,1)} %copy-done.4) | copy-start | bytes 9437188
  393.7 13.1 %all-to-all-start.12 = ((bf16[2,128,768]{1,0,2:T(2,128)(2,1)}), bf16[2,128,768]{1,0,2:T(2,128)(2,1)}, u32[]{:S(2)}, u32[]{:S(2)}) async-start(bf16[2,128,768]{1,0,2:T(2,128)(2,1)} %copy.398), calls=%async_computation.12 | async-start | bytes 786432 | tf_op jit(solution)/shard_map/all_to_all | solution.py:159
  447.7 38.1 %all-to-all-start.13 = ((bf16[2,512,3,192]{3,0,2,1:T(2,128)(2,1)}), bf16[2,512,3,192]{3,0,2,1:T(2,128)(2,1)S(1)}, u32[]{:S(2)}, u32[]{:S(2)}) async-start(bf16[2,512,3,192]{3,0,2,1:T(2,128)(2,1)} %pad_maximum_fusion), calls=%async_computation.13 | async-start | bytes 3145728 | tf_op jit(solution)/shard_map/all_to_all | solution.py:191
  481.0 9.3 copy-start.20
  485.9 29.6 %all-to-all-start.15 = ((bf16[2,512,3,192]{3,0,2,1:T(2,128)(2,1)}), bf16[2,512,3,192]{3,0,2,1:T(2,128)(2,1)}, u32[]{:S(2)}, u32[]{:S(2)}) async-start(bf16[2,512,3,192]{3,0,2,1:T(2,128)(2,1)} %pad_maximum_fusion.1), calls=%async_computation.15 | async-start | bytes 3145728 | tf_op jit(solution)/shard_map/all_to_all | solution.py:191
  490.2 201.4 %reduce-scatter.8.cloned.1.call-start = ((), (), s32[]{:S(2)}) async-start(), calls=%async_computation.23 | async-start | bytes 7962624 | tf_op jit(solution)/shard_map/reduce_scatter | solution.py:301
  529.1 294.5 %reduce-scatter.12.cloned.1.call-start = ((), (), s32[]{:S(2)}) async-start(), calls=%async_computation.25 | async-start | bytes 10616832 | tf_op jit(solution)/shard_map/reduce_scatter | solution.py:303
  539.1 451.0 %reduce-scatter.14.cloned.1.call-start = ((), (), s32[]{:S(2)}) async-start(), calls=%async_computation.26 | async-start | bytes 10616832 | tf_op jit(solution)/shard_map/reduce_scatter | solution.py:304
  549.4 13.8 %copy-start.97 = (f32[768]{0:T(1024)S(1)}, f32[768]{0:T(1024)}, u32[]{:S(2)}) copy-start(f32[768]{0:T(1024)} %get-tuple-element.43) | copy-start | bytes 9220
  549.4 14.4 %copy-start.96 = (f32[768]{0:T(1024)S(1)}, f32[768]{0:T(1024)}, u32[]{:S(2)}) copy-start(f32[768]{0:T(1024)} %get-tuple-element.44) | copy-start | bytes 9220
  549.5 14.9 %copy-start.99 = (f32[768]{0:T(1024)S(1)}, f32[768]{0:T(1024)}, u32[]{:S(2)}) copy-start(f32[768]{0:T(1024)} %get-tuple-element.51) | copy-start | bytes 9220
  549.5 15.5 %copy-start.98 = (f32[768]{0:T(1024)S(1)}, f32[768]{0:T(1024)}, u32[]{:S(2)}) copy-start(f32[768]{0:T(1024)} %get-tuple-element.160) | copy-start | bytes 9220
  559.1 48.9 %all-to-all-start.3 = ((bf16[4,2,24576]{2,1,0:T(2,128)(2,1)}), bf16[4,2,24576]{2,1,0:T(2,128)(2,1)}, u32[]{:S(2)}, u32[]{:S(2)}) async-start(bf16[4,2,24576]{2,1,0:T(2,128)(2,1)} %reshape.979), calls=%async_computation.3 | async-start | bytes 786432 | tf_op jit(solution)/shard_map/all_to_all | solution.py:287
  565.0 23.2 %copy-start.100 = (f32[768]{0:T(1024)S(1)}, f32[768]{0:T(1024)}, u32[]{:S(2)}) copy-start(f32[768]{0:T(1024)} %get-tuple-element.108) | copy-start | bytes 9220
  608.0 16.1 %all-to-all-start.1 = ((bf16[4,2,24576]{2,1,0:T(2,128)(2,1)}), bf16[4,2,24576]{2,1,0:T(2,128)(2,1)}, u32[]{:S(2)}, u32[]{:S(2)}) async-start(bf16[4,2,24576]{2,1,0:T(2,128)(2,1)} %reshape.981), calls=%async_computation.1 | async-start | bytes 786432 | tf_op jit(solution)/shard_map/all_to_all | solution.py:287
  624.0 15.8 %all-to-all-start.11 = ((bf16[4,2,24576]{2,1,0:T(2,128)(2,1)}), bf16[4,2,24576]{2,1,0:T(2,128)(2,1)}, u32[]{:S(2)}, u32[]{:S(2)}) async-start(bf16[4,2,24576]{2,1,0:T(2,128)(2,1)} %reshape.983), calls=%async_computation.11 | async-start | bytes 786432 | tf_op jit(solution)/shard_map/all_to_all | solution.py:288
  631.8 18.9 %copy-start.105 = (f32[768,1]{0,1:T(1,128)S(1)}, f32[768,1]{0,1:T(1,128)}, u32[]{:S(2)}) copy-start(f32[768,1]{0,1:T(1,128)} %stack.211) | copy-start | bytes 9220
  639.8 31.4 %all-to-all-start.9 = ((bf16[4,2,24576]{2,1,0:T(2,128)(2,1)}), bf16[4,2,24576]{2,1,0:T(2,128)(2,1)}, u32[]{:S(2)}, u32[]{:S(2)}) async-start(bf16[4,2,24576]{2,1,0:T(2,128)(2,1)} %reshape.985), calls=%async_computation.9 | async-start | bytes 786432 | tf_op jit(solution)/shard_map/all_to_all | solution.py:288
  644.0 410.8 %reduce-scatter.16.cloned.1.call-start = ((), (), s32[]{:S(2)}) async-start(), calls=%async_computation.27 | async-start | bytes 442368
  685.2 419.7 %all-reduce.3.cloned.1.call-start = ((), (), s32[]{:S(2)}) async-start(), calls=%async_computation.28 | async-start | bytes 3538944 | tf_op jit(solution)/shard_map/psum | solution.py:310
  992.2 69.0 %copy-start.89 = (f32[96,12]{0,1:T(8,128)S(1)}, f32[96,12]{0,1:T(8,128)}, u32[]{:S(2)}) copy-start(f32[96,12]{0,1:T(8,128)} %param.23) | copy-start | bytes 13828
  992.3 70.3 %copy-start.118 = (f32[96,12]{0,1:T(8,128)S(1)}, f32[96,12]{0,1:T(8,128)}, u32[]{:S(2)}) copy-start(f32[96,12]{0,1:T(8,128)} %param.29) | copy-start | bytes 13828
  992.3 112.7 %copy-start.29 = (f32[384,768]{1,0:T(8,128)S(1)}, f32[384,768]{1,0:T(8,128)}, u32[]{:S(2)}) copy-start(f32[384,768]{1,0:T(8,128)} %param.22) | copy-start | bytes 3538948
  992.3 112.6 %copy-start.38 = (f32[384,768]{1,0:T(8,128)S(1)}, f32[384,768]{1,0:T(8,128)}, u32[]{:S(2)}) copy-start(f32[384,768]{1,0:T(8,128)} %param.25) | copy-start | bytes 3538948
  1062.6 45.5 %copy-start.87 = (f32[96,12]{0,1:T(8,128)}, f32[96,12]{0,1:T(8,128)S(1)}, u32[]{:S(2)}) copy-start(f32[96,12]{0,1:T(8,128)S(1)} %get-tuple-element.66) | copy-start | bytes 13828
  (113 other events, 397.2 us)
Sparse Core Ops, SparseCore 0:
  10.8 141.1 all-gather.2
  154.8 78.0 all-gather.4
  377.2 67.9 reduce-scatter.9
  529.2 128.0 reduce-scatter.7
  661.2 162.3 reduce-scatter.11
  827.5 162.5 reduce-scatter.13
  994.3 60.4 reduce-scatter.15
  1059.3 45.6 all-reduce.2
